TPU v7x, 256 devices: a whole 4x4x8 slice. The times are simulated.
256 devices in a mesh: dp: 32 (over z, y), tp: 8 (over x, core).
Axes of the slice: x: 4, y: 4, z: 8, core: 2. Of those that a mesh axis runs over, the one named last changes fastest.
Arguments:
- tokens: bfloat16 [16384, 2560], P('dp', 'tp'), may hold values from -20 to 20
- pre_act: bfloat16 [16384, 10240], P('dp', 'tp'), may hold values from -6 to 6
- act_grad: bfloat16 [16384, 10240], P('dp', 'tp'), may hold values from -3 to 3
Outputs:
- slab_gradient: bfloat16 [2560, 10240], P(None, 'tp')
All inputs are finite; a program needn't handle non-finite values.
Results may differ from a plain program's by a relative error of at most 0.0052.
Values may be sent and summed in bfloat16 or wider, within the bound.
A program may use at most 64 MiB of HBM per device.

v0:
```python
import jax
import jax.numpy as jnp
from jax import lax
from jax.sharding import PartitionSpec as P

norm_epsilon = 1e-06
gelu_scale = 0.7978845608


def swapped(block, axis, stride):
    count = lax.axis_size(axis)
    route = []
    for low in range(count):
        high = low | 1 << stride
        if high != low and high < count:
            route += [(low, high), (high, low)]
    return lax.ppermute(block, axis, route)


def gelu_slope(values):
    inner = gelu_scale * (values + 0.044715 * values * values * values)
    tangent = jnp.tanh(inner)
    return 0.5 * (1.0 + tangent) + 0.5 * values * (1.0 - tangent * tangent) * gelu_scale * (
        1.0 + 0.134145 * values * values
    )


def on_device(tokens, pre_act, act_grad):
    derivative = gelu_slope(pre_act.astype(jnp.float32))
    grad_pre = (act_grad.astype(jnp.float32) * derivative).astype(jnp.bfloat16)
    holding = lax.dot_general(
        lax.all_gather(tokens, "tp", axis=1, tiled=True),
        grad_pre,
        (((0,), (0,)), ((), ())),
        preferred_element_type=jnp.float32,
    ).astype(jnp.bfloat16)
    replicas = lax.axis_size("dp")
    levels = replicas.bit_length() - 1
    my_index = lax.axis_index("dp")
    split_axis = 0
    for section_index in range(levels):
        bit_index = levels - 1 - section_index
        is_lower = my_index >> bit_index & 1 == 0
        half_length = holding.shape[split_axis] // 2
        front_half = lax.slice_in_dim(holding, 0, half_length, axis=split_axis)
        back_half = lax.slice_in_dim(holding, half_length, 2 * half_length, axis=split_axis)
        retained = jnp.where(is_lower, front_half, back_half)
        outgoing = jnp.where(is_lower, back_half, front_half)
        arrived = swapped(outgoing, "dp", bit_index)
        lower_part = jnp.where(is_lower, retained, arrived).astype(jnp.float32)
        upper_part = jnp.where(is_lower, arrived, retained).astype(jnp.float32)
        partial_value = jnp.stack(
            [
                jnp.sum(lower_part * upper_part),
                jnp.sum(lower_part * lower_part),
                jnp.sum(upper_part * upper_part),
            ]
        )
        group_count = 1 << bit_index
        membership = (jnp.arange(group_count) == my_index % group_count).astype(jnp.float32)
        table = partial_value[:, None] * membership[None, :]
        summed = lax.psum(table, ("dp", "tp"))
        totals = jnp.sum(summed * membership[None, :], axis=1)
        lower_coef = 1.0 - totals[0] / (2.0 * (totals[1] + norm_epsilon))
        upper_coef = 1.0 - totals[0] / (2.0 * (totals[2] + norm_epsilon))
        holding = (lower_coef * lower_part + upper_coef * upper_part).astype(jnp.bfloat16)
    combined = lax.all_gather(holding, "dp", axis=0, tiled=True)
    return combined


def solution(mesh):
    return jax.shard_map(
        on_device,
        mesh=mesh,
        in_specs=(P("dp", "tp"), P("dp", "tp"), P("dp", "tp")),
        out_specs=P(None, "tp"),
        check_vma=False,
    )
```

profile of v0, /device:TPU:1, one launch (start us, length us, event | category | flops | bytes accessed | tf_op | source)
XLA Modules:
  0.0 843.0 jit_solution(3903587580465807351)
XLA Ops:
  6.5 0.7 all-gather.3.cloned.1.call-update
  7.3 34.8 %all-gather.3.cloned.1.call-done = bf16[512,2560]{0,1:T(8,128)(2,1)} async-done(((bf16[512,320]{0,1:T(8,128)(2,1)}), bf16[512,2560]{0,1:T(8,128)(2,1)}) %all-gather.3.cloned.1.call-update) | async-done | bytes 2621456 | tf_op jit(solution)/shard_map/all_gather | solution.py:32
  42.1 7.7 fusion
  49.8 0.3 broadcast_select_fusion.2
  50.1 2.5 copy-done
  52.6 5.5 collective-permute-start
  58.0 142.7 %collective-permute-done = bf16[1280,1280]{0,1:T(8,128)(2,1)} collective-permute-done((bf16[1280,1280]{0,1:T(8,128)(2,1)S(1)}, bf16[1280,1280]{0,1:T(8,128)(2,1)}, u32[]{:S(2)}, u32[]{:S(2)}) %collective-permute-start) | collective-permute-done | bytes 3276832 | tf_op jit(solution)/shard_map/ppermute | solution.py:17
  200.7 7.6 fusion.4
  208.3 1.9 pad_maximum_fusion
  210.2 75.5 %psum.35 = f32[3,16]{1,0:T(4,128)S(1)} all-reduce(f32[3,16]{1,0:T(4,128)S(1)} %broadcast_multiply_fusion.2), channel_id=1, replica_groups=mesh['dp'=32,'tp'=8] {'dp','tp'}, use_global_device_ids=true, to_apply=%region_3.4 | all-reduce | flops 48 | bytes 384 | tf_op jit(solution)/shard_map/psum | solution.py:62
  285.9 0.7 fusion.50
  289.0 4.1 fusion.3
  293.2 1.3 broadcast_select_fusion.6
  294.5 2.1 collective-permute-start.1
  296.6 70.9 %collective-permute-done.1 = bf16[640,1280]{0,1:T(8,128)(2,1)} collective-permute-done((bf16[640,1280]{0,1:T(8,128)(2,1)}, bf16[640,1280]{0,1:T(8,128)(2,1)}, u32[]{:S(2)}, u32[]{:S(2)}) %collective-permute-start.1) | collective-permute-done | bytes 1638432 | tf_op jit(solution)/shard_map/ppermute | solution.py:17
  367.5 4.4 fusion.9
  371.9 1.9 pad_maximum_fusion.1
  373.9 75.3 %psum.36 = f32[3,8]{1,0:T(4,128)S(1)} all-reduce(f32[3,8]{1,0:T(4,128)S(1)} %broadcast_multiply_fusion.1), channel_id=1, replica_groups=mesh['dp'=32,'tp'=8] {'dp','tp'}, use_global_device_ids=true, to_apply=%region_8.9 | all-reduce | flops 24 | bytes 192 | tf_op jit(solution)/shard_map/psum | solution.py:62
  449.4 0.7 fusion.49
  452.5 2.5 fusion.8
  455.1 0.4 broadcast_select_fusion.10
  455.5 0.6 copy.12
  456.2 19.2 %collective-permute-done.2 = bf16[320,1280]{1,0:T(8,128)(2,1)} collective-permute-done((bf16[320,1280]{1,0:T(8,128)(2,1)S(1)}, bf16[320,1280]{1,0:T(8,128)(2,1)}, u32[]{:S(2)}, u32[]{:S(2)}) %collective-permute-start.2) | collective-permute-done | bytes 819232 | tf_op jit(solution)/shard_map/ppermute | solution.py:17
  475.4 1.5 copy.13
  476.9 3.1 fusion.23
  480.1 1.9 pad_maximum_fusion.2
  482.0 74.2 %psum.37 = f32[3,4]{1,0:T(4,128)S(1)} all-reduce(f32[3,4]{1,0:T(4,128)S(1)} %broadcast_multiply_fusion), channel_id=1, replica_groups=mesh['dp'=32,'tp'=8] {'dp','tp'}, use_global_device_ids=true, to_apply=%region_13.14 | all-reduce | flops 12 | bytes 96 | tf_op jit(solution)/shard_map/psum | solution.py:62
  556.3 0.7 fusion.48
  559.4 1.9 fusion.22
  561.2 0.2 broadcast_select_fusion.14
  561.5 0.2 copy.15
  561.7 1.2 collective-permute-start.3
  562.9 10.7 %collective-permute-done.3 = bf16[160,1280]{1,0:T(8,128)(2,1)S(1)} collective-permute-done((bf16[160,1280]{1,0:T(8,128)(2,1)S(1)}, bf16[160,1280]{1,0:T(8,128)(2,1)S(1)}, u32[]{:S(2)}, u32[]{:S(2)}) %collective-permute-start.3) | collective-permute-done | bytes 409632 | tf_op jit(solution)/shard_map/ppermute | solution.py:17
  573.6 0.2 copy.16
  573.9 1.5 fusion.29
  575.4 2.0 pad_maximum_fusion.3
  577.4 73.7 %psum.38 = f32[3,2]{0,1:T(2,128)S(1)} all-reduce(f32[3,2]{0,1:T(2,128)S(1)} %broadcast_multiply_fusion.3), channel_id=1, replica_groups=mesh['dp'=32,'tp'=8] {'dp','tp'}, use_global_device_ids=true, to_apply=%region_18.19 | all-reduce | flops 6 | bytes 48 | tf_op jit(solution)/shard_map/psum | solution.py:62
  651.2 0.7 fusion.47
  654.4 0.3 fusion.28
  654.8 0.5 collective-permute-start.4
  655.3 8.2 collective-permute-done.4
  663.5 1.1 fusion.39
  664.6 2.0 pad_maximum_fusion.4
  666.6 74.0 %psum.39 = f32[3,1]{0,1:T(1,128)S(1)} all-reduce(f32[3,1]{0,1:T(1,128)S(1)} %pad_maximum_fusion.4), channel_id=1, replica_groups=mesh['dp'=32,'tp'=8] {'dp','tp'}, use_global_device_ids=true, to_apply=%region_23.24 | all-reduce | flops 3 | bytes 24 | tf_op jit(solution)/shard_map/psum | solution.py:62
  740.5 0.7 fusion.46
  743.8 0.8 copy.18
  744.7 85.5 %all-gather.5.cloned.1.call-done = bf16[2560,1280]{1,0:T(8,128)(2,1)} async-done(((bf16[80,1280]{1,0:T(8,128)(2,1)}), bf16[2560,1280]{1,0:T(8,128)(2,1)}) %all-gather.5.cloned.1.call-update) | async-done | bytes 6553616 | tf_op jit(solution)/shard_map/all_gather | solution.py:67
  830.1 6.1 copy.20
  (19 shorter events, 1.2 us)
Async XLA Ops:
  6.5 35.6 %all-gather.3.cloned.1.call-start = ((), (), s32[]{:S(2)}) async-start(), calls=%async_computation | async-start | bytes 2949120 | tf_op jit(solution)/shard_map/all_gather | solution.py:32
  7.3 822.9 %all-gather.5.cloned.1.call-start = ((), (), s32[]{:S(2)}) async-start(), calls=%async_computation.1 | async-start | bytes 6758400 | tf_op jit(solution)/shard_map/all_gather | solution.py:67
  49.8 2.8 copy-start
  52.6 148.1 %collective-permute-start = (bf16[1280,1280]{0,1:T(8,128)(2,1)S(1)}, bf16[1280,1280]{0,1:T(8,128)(2,1)}, u32[]{:S(2)}, u32[]{:S(2)}) collective-permute-start(bf16[1280,1280]{0,1:T(8,128)(2,1)S(1)} %broadcast_select_fusion.2), channel_id=1, source_target_pairs={{0,128},{128,0},{8,136},{136,8},{16,144},{144,16},{24,152},{152,24... | collective-permute-start | bytes 9830408 | tf_op jit(solution)/shard_map/ppermute | solution.py:17
  294.5 73.0 %collective-permute-start.1 = (bf16[640,1280]{0,1:T(8,128)(2,1)}, bf16[640,1280]{0,1:T(8,128)(2,1)}, u32[]{:S(2)}, u32[]{:S(2)}) collective-permute-start(bf16[640,1280]{0,1:T(8,128)(2,1)} %broadcast_select_fusion.6), channel_id=1, source_target_pairs={{0,64},{64,0},{8,72},{72,8},{16,80},{80,16},{24,88},{88,24},{32,96... | collective-permute-start | bytes 4915208 | tf_op jit(solution)/shard_map/ppermute | solution.py:17
  456.1 19.3 %collective-permute-start.2 = (bf16[320,1280]{1,0:T(8,128)(2,1)S(1)}, bf16[320,1280]{1,0:T(8,128)(2,1)}, u32[]{:S(2)}, u32[]{:S(2)}) collective-permute-start(bf16[320,1280]{1,0:T(8,128)(2,1)S(1)} %copy.12), channel_id=1, source_target_pairs={{0,32},{32,0},{8,40},{40,8},{16,48},{48,16},{24,56},{56,24},{64,96... | collective-permute-start | bytes 2457608 | tf_op jit(solution)/shard_map/ppermute | solution.py:17
  561.7 11.9 %collective-permute-start.3 = (bf16[160,1280]{1,0:T(8,128)(2,1)S(1)}, bf16[160,1280]{1,0:T(8,128)(2,1)S(1)}, u32[]{:S(2)}, u32[]{:S(2)}) collective-permute-start(bf16[160,1280]{1,0:T(8,128)(2,1)S(1)} %copy.15), channel_id=1, source_target_pairs={{0,16},{16,0},{8,24},{24,8},{32,48},{48,32},{40,56},{56,40},{64,80... | collective-permute-start | bytes 1228808 | tf_op jit(solution)/shard_map/ppermute | solution.py:17
  654.8 8.7 %collective-permute-start.4 = (bf16[80,1280]{0,1:T(8,128)(2,1)S(1)}, bf16[80,1280]{0,1:T(8,128)(2,1)S(1)}, u32[]{:S(2)}, u32[]{:S(2)}) collective-permute-start(bf16[80,1280]{0,1:T(8,128)(2,1)S(1)} %broadcast_select_fusion.18), channel_id=1, source_target_pairs={{0,8},{8,0},{16,24},{24,16},{32,40},{40,32},{48,56},{56,48},{64,72... | collective-permute-start | bytes 614408 | tf_op jit(solution)/shard_map/ppermute | solution.py:17
Sparse Core Ops, SparseCore 0:
  9.2 32.8 all-gather.2
  744.8 85.2 all-gather.4
where the time goes:
time: 844 us; the launch traced here: 843 us
  waiting for transfers between devices  373 us (44%)
  blocking collectives  373 us (44%)
  other arithmetic  39.5 us (5%)
  between operations  25.9 us (3%)
  local copies, waits for them, and re-layouts  15.3 us (2%)
  starting transfers between devices  9.38 us (1%)
    psum x5, blocking collectives, on_device(): summed = lax.psum(table, ('dp', 'tp'))  373 us
    ppermute x5, waiting for transfers between devices, swapped(): return lax.ppermute(block, axis, route)  252 us
    all_gather x1, waiting for transfers between devices, on_device(): combined = lax.all_gather(holding, 'dp', axis=0, tiled=True)  85.5 us
    all_gather x1, waiting for transfers between devices, on_device(): lax.all_gather(tokens, 'tp', axis=1, tiled=True)  34.8 us
    reduce_sum x5, other arithmetic, on_device(): jnp.sum(lower_part * upper_part)  17.8 us
  transfers between devices with their start and end apart: 7, of which 7 were waited for; matrix products, arithmetic and copies ran while one was open for 0% of the time, Pallas kernels for 0%

commit v1 on v0

v1 whole, which is shorter than its diff:
```python
import jax
import jax.numpy as jnp
from jax import lax
from jax.experimental import pallas as pl
from jax.experimental.pallas import tpu as pltpu
from jax.sharding import PartitionSpec as P

norm_epsilon = 1e-06
gelu_scale = 0.7978845608
MESH = pl.DeviceIdType.MESH
NX, NY, NZ = 4, 4, 8
SEND_SEMS = 192


def gelu_slope(values):
    inner = gelu_scale * (values + 0.044715 * values * values * values)
    tangent = jnp.tanh(inner)
    return 0.5 * (1.0 + tangent) + 0.5 * values * (1.0 - tangent * tangent) * gelu_scale * (
        1.0 + 0.134145 * values * values
    )


def signed(step):
    return step if step <= NZ // 2 else step - NZ


def tree_weights(gram, strides):
    shape = gram.shape
    row = lax.broadcasted_iota(jnp.int32, shape, 0)
    lane = lax.broadcasted_iota(jnp.int32, shape, 1)
    own = lane % 8 == row
    first = lane < 8
    weight = jnp.ones((8, 1), jnp.float32)
    for stride in strides:
        pair = lane % 8 == (row + stride) % 8
        own_col = jnp.sum(jnp.where(own & first, gram, 0.0), axis=1, keepdims=True)
        pair_col = jnp.sum(jnp.where(pair & first, gram, 0.0), axis=1, keepdims=True)
        own_row = jnp.sum(jnp.where(own, gram, 0.0), axis=0, keepdims=True)
        pair_row = jnp.sum(
            jnp.where(row == (lane + stride) % 8, gram, 0.0), axis=0, keepdims=True
        )
        coef_col = 1.0 - pair_col / (2.0 * (jnp.maximum(own_col, 0.0) + norm_epsilon))
        coef_row = 1.0 - pair_row / (2.0 * (jnp.maximum(own_row, 0.0) + norm_epsilon))
        weight = weight * coef_col
        scaled = gram * coef_col * coef_row
        scaled = scaled + pltpu.roll(scaled, stride, 0)
        gram = scaled + pltpu.roll(scaled, stride, 1)
    return weight


def fold_gram(product, count, group):
    size = count * group
    row = lax.broadcasted_iota(jnp.int32, (size, size), 0)
    lane = lax.broadcasted_iota(jnp.int32, (size, size), 1)
    kept = jnp.where(row % group == lane % group, product, 0.0)
    rows = jnp.sum(kept.reshape(count, group, size), axis=1)
    lane = lax.broadcasted_iota(jnp.int32, (count, size), 1)
    out_lane = lax.broadcasted_iota(jnp.int32, (count, 128), 1)
    total = jnp.zeros((count, 128), jnp.float32)
    for index in range(count):
        one = jnp.sum(jnp.where(lane // group == index, rows, 0.0), axis=1, keepdims=True)
        total = jnp.where(out_lane % count == index, one, total)
    return total


def kernel(
    xt, pre, act, out,
    xb, yb, ys, pre_v, act_v, grads, prod, vs, vr, fin,
    a1, a2, b1, b2,
    load_sem, send_sem, xz_sem, xx_sem, yz_sem, yy_sem, v_sem, ar_sem,
    bz_sem, by_sem, az_sem, ay_sem,
):
    dp, tp = lax.axis_index("dp"), lax.axis_index("tp")
    z, y, x, c = dp // NY, dp % NY, tp // 2, tp % 2
    tokens = yb.shape[1]
    half_tok = tokens // 2
    feats = xb.shape[2]
    cols = yb.shape[2]

    def dev(x_, c_, y_, z_):
        return (z_ * NY + y_, x_ * 2 + c_)

    def zn(step):
        return (z + step + NZ) % NZ

    def yn(step):
        return (y + step + NY) % NY

    def xn(step):
        return (x + step + NX) % NX

    pending = []
    counter = [0]

    def send(src, dst, recv, device, cond=None, size=None):
        copy = pltpu.make_async_remote_copy(
            src_ref=src, dst_ref=dst, send_sem=send_sem.at[counter[0]], recv_sem=recv,
            device_id=device, device_id_type=MESH,
        )
        if cond is None:
            copy.start()
        else:
            pl.when(cond)(copy.start)
        pending.append((size or (lambda: src), counter[0], cond))
        counter[0] += 1

    def arrived(ref, sem):
        pltpu.make_async_copy(ref, ref, sem).wait()

    def drain(items):
        for ref, index, cond in items:
            if cond is None:
                arrived(ref(), send_sem.at[index])
            else:
                pl.when(cond)(lambda: arrived(ref(), send_sem.at[index]))

    loads = [
        pltpu.make_async_copy(pre, pre_v, load_sem.at[0]),
        pltpu.make_async_copy(act, act_v, load_sem.at[1]),
    ]
    for load in loads:
        load.start()

    barrier = pltpu.get_barrier_semaphore()
    partners = [dev(x, k, y, zn(s)) for s in range(1, NZ) for k in range(2)]
    partners += [dev(x, 1 - c, y, z)]
    partners += [dev(xn(s), k, y, z) for s in range(1, NX) for k in range(2)]
    partners += [dev(x, k, yn(s), z) for s in range(1, NY) for k in range(2)]
    partners += [dev(xn(s), c, yn(t), z) for s in range(1, NX) for t in range(1, NY)]
    for partner in partners:
        pl.semaphore_signal(barrier, inc=1, device_id=partner, device_id_type=MESH)
    pl.semaphore_wait(barrier, len(partners))

    match = z % 2 == c
    reach = jnp.where(match, 2, 1)
    for sign in (1, -1):
        for k in range(2):
            send(
                xt.at[pl.ds(k * feats, feats)], xb.at[z, x], xz_sem.at[z],
                dev(x, k, y, (z + sign * reach + NZ) % NZ),
            )
    other = pl.multiple_of((1 - c) * feats, 16)
    mine = pl.multiple_of(c * feats, 16)
    own_x = pltpu.make_async_copy(xt.at[pl.ds(mine, feats)], xb.at[z, x], xz_sem.at[z])
    pl.when(match)(own_x.start)
    send(xt.at[pl.ds(other, feats)], xb.at[z, x], xz_sem.at[z], dev(x, 1 - c, y, z), match)

    for load in loads:
        load.wait()
    chunk = 32
    my_pair, my_parity = z // 2, z % 2
    for j in range(2):
        def slope_rows(i, carry):
            rows = pl.ds(pl.multiple_of(i * chunk, chunk), chunk)
            span = pl.ds(j * cols, cols)
            slope = gelu_slope(pre_v[rows, span].astype(jnp.float32))
            ys[j, rows, :] = (act_v[rows, span].astype(jnp.float32) * slope).astype(jnp.bfloat16)
            return carry

        lax.fori_loop(0, tokens // chunk, slope_rows, 0)
        quarter = 2 * c + j
        ahead = (quarter - my_pair + 4) % 4
        upper = jnp.where(
            ahead == 0, 1 - my_parity,
            jnp.where(ahead == 3, 1, jnp.where(ahead == 2, 1 - my_parity, 0)),
        )
        target = 2 * quarter + upper
        for k in range(2):
            rows = pl.ds(k * half_tok, half_tok)
            send(ys.at[j, rows], yb.at[z, rows], yz_sem.at[z], dev(x, k, y, target))
        own = ahead == 0
        own_rows = pl.ds(pl.multiple_of(c * half_tok, 16), half_tok)
        other_rows = pl.ds(pl.multiple_of((1 - c) * half_tok, 16), half_tok)
        own_y = pltpu.make_async_copy(ys.at[j, own_rows], yb.at[z, own_rows], yz_sem.at[z])
        pl.when(own)(own_y.start)
        send(ys.at[j, other_rows], yb.at[z, other_rows], yz_sem.at[z], dev(x, 1 - c, y, z), own)

    def ev_xz(step):
        src = zn(-step)
        piece = xb.at[src, x]
        arrived(piece, xz_sem.at[src])
        if step == 1:
            send(piece, piece, xz_sem.at[src], dev(x, c, y, zn(2)))
        if step == -1:
            send(piece, piece, xz_sem.at[src], dev(x, c, y, zn(-2)))
        if step == 2:
            send(piece, piece, xz_sem.at[src], dev(x, c, y, zn(2)), c == 0)
        if step == -2:
            send(piece, piece, xz_sem.at[src], dev(x, c, y, zn(-2)), c == 1)
        send(piece, piece, xx_sem.at[src, 0], dev(xn(1), c, y, z))
        send(piece, piece, xx_sem.at[src, 1], dev(xn(-1), c, y, z))

    low, high = pl.ds(0, feats // 2), pl.ds(feats // 2, feats // 2)

    def ev_xx(step):
        src = zn(-step)
        left, right = xb.at[src, xn(-1)], xb.at[src, xn(1)]
        arrived(left, xx_sem.at[src, 0])
        send(left.at[low], left.at[low], xx_sem.at[src, 2], dev(xn(1), c, y, z))
        arrived(right, xx_sem.at[src, 1])
        send(right.at[high], right.at[high], xx_sem.at[src, 3], dev(xn(-1), c, y, z))

    my_tok = pl.ds(pl.multiple_of(c * half_tok, 16), half_tok)
    its_tok = pl.ds(pl.multiple_of((1 - c) * half_tok, 16), half_tok)

    def ev_yz(step):
        src = zn(-step)
        piece = yb.at[src, my_tok]
        arrived(piece, yz_sem.at[src])
        if step in (1, 2, 3):
            send(piece, piece, yz_sem.at[src], dev(x, c, y, zn(1)), z % 2 == 0)
        if step in (-1, -2, -3):
            send(piece, piece, yz_sem.at[src], dev(x, c, y, zn(-1)), z % 2 == 1)
        send(piece, piece, yy_sem.at[src], dev(x, 1 - c, y, z))

    def ev_mm(step):
        src = zn(-step)
        far = xb.at[src, xn(2)]
        arrived(far.at[low], xx_sem.at[src, 2])
        arrived(far.at[high], xx_sem.at[src, 3])
        arrived(yb.at[src, its_tok], yy_sem.at[src])

        def block(i, carry):
            result = jnp.dot(xb[src, i], yb[src], preferred_element_type=jnp.float32)
            grads[src, pl.ds(pl.multiple_of(i * feats, 16), feats), :] = result.astype(jnp.bfloat16)
            return carry

        lax.fori_loop(0, NX, block, 0)

    xz, xx, yz, mm = ev_xz, ev_xx, ev_yz, ev_mm
    for event, step in [
        (xz, 0), (xz, 1), (xz, -1), (xx, 0), (xz, 2), (xz, -2), (xx, 1), (xx, -1),
        (yz, 0), (yz, 1), (yz, -1), (xx, 2), (xx, -2), (xz, 3), (xz, -3), (xz, 4), (mm, 0),
        (yz, 2), (yz, -2), (xx, 3), (xx, -3), (mm, 1), (mm, -1), (yz, 3), (yz, -3), (xx, 4),
        (mm, 2), (mm, -2), (yz, 4), (mm, 3), (mm, -3), (mm, 4),
    ]:
        event(step)

    group = 32
    total_rows = grads.shape[1]
    prod[...] = jnp.zeros_like(prod)

    def gram_rows(i, carry):
        rows = pl.ds(pl.multiple_of(i * group, group), group)
        stacked = grads[:, rows, :].reshape(NZ * group, cols)
        prod[...] += lax.dot_general(
            stacked, stacked, (((1,), (1,)), ((), ())), preferred_element_type=jnp.float32
        )
        return carry

    lax.fori_loop(0, total_rows // group, gram_rows, 0)
    a1[tp] = fold_gram(prod[...], NZ, group)
    for s in range(1, 2 * NX):
        send(a1.at[tp], a1.at[tp], ar_sem.at[0], (dp, (tp + s) % (2 * NX)))
    sent = pl.ds(0, 2 * NX - 1)
    arrived(a1.at[sent], ar_sem.at[0])
    a2[z] = jnp.sum(a1[...], axis=0)
    for s in range(1, NZ):
        send(a2.at[z], a2.at[z], ar_sem.at[1], dev(x, c, y, zn(s)))
    drain(pending)
    pending.clear()
    arrived(a2.at[pl.ds(0, NZ - 1)], ar_sem.at[1])
    weight = tree_weights(jnp.sum(a2[...], axis=0), (4, 2, 1))

    owner = z // 4
    is_owner = c == owner
    its_rows = pl.ds(pl.multiple_of(c * feats, 16), feats)
    small = 32
    for s in (1, -1, 2, 0):
        part = yn(s)

        def combine_rows(i, carry):
            total = jnp.zeros((small, cols), jnp.float32)
            rows = pl.ds(pl.multiple_of(part * feats + i * small, 32), small)
            for r in range(NZ):
                total += weight[r:r + 1, :] * grads[r, rows, :].astype(jnp.float32)
            vs[part, pl.ds(pl.multiple_of(i * small, small), small), :] = total.astype(jnp.bfloat16)
            return carry

        lax.fori_loop(0, feats // small, combine_rows, 0)
        if s:
            send(vs.at[part], vr.at[y, its_rows], v_sem.at[y, c], dev(x, owner, part, z))
        else:
            own_v = pltpu.make_async_copy(vs.at[part], vr.at[y, its_rows], v_sem.at[y, c])
            pl.when(is_owner)(own_v.start)
            send(vs.at[part], vr.at[y, its_rows], v_sem.at[y, c], dev(x, owner, part, z),
                 jnp.logical_not(is_owner))

    block_rows = 2 * feats
    cut = block_rows * 2 // 5
    part_a, part_b = (0, cut), (cut, block_rows - cut)

    def place(y_, z_, start, size):
        top = pl.multiple_of((2 * y_ + z_ % 2) * block_rows + start, 16)
        left = pl.multiple_of((z_ // 2) % 2 * cols, 128)
        return out.at[pl.ds(top, size), pl.ds(left, cols)]

    def halves(part):
        start, size = part
        return (start, size // 2), (start + size // 2, size // 2)

    def finish():
        for src in range(NY):
            for k in range(2):
                arrived(vr.at[src, pl.ds(k * feats, feats)], v_sem.at[src, k])
        size = NY * group
        prod[0:size, 0:size] = jnp.zeros((size, size), jnp.float32)

        def gram(i, carry):
            rows = pl.ds(pl.multiple_of(i * group, group), group)
            stacked = vr[:, rows, :].reshape(size, cols)
            prod[0:size, 0:size] += lax.dot_general(
                stacked, stacked, (((1,), (1,)), ((), ())), preferred_element_type=jnp.float32
            )
            return carry

        lax.fori_loop(0, block_rows // group, gram, 0)
        folded = fold_gram(prod[0:size, 0:size], NY, group)
        me = x * NY + y
        b1[me] = jnp.concatenate([folded, folded], axis=0)
        for s in range(NX):
            for t in range(NY):
                if s or t:
                    send(b1.at[me], b1.at[me], ar_sem.at[2], dev(xn(s), c, yn(t), z), size=lambda: b1.at[0])
        arrived(b1.at[pl.ds(0, NX * NY - 1)], ar_sem.at[2])
        b2[z] = jnp.sum(b1[...], axis=0)
        for s in range(1, NZ):
            send(b2.at[z], b2.at[z], ar_sem.at[3], dev(x, zn(s) // 4, y, zn(s)), size=lambda: b2.at[0])
        arrived(b2.at[pl.ds(0, NZ - 1)], ar_sem.at[3])
        last = tree_weights(jnp.sum(b2[...], axis=0), (2, 1))

        def final_rows(i, carry):
            total = jnp.zeros((small, cols), jnp.float32)
            rows = pl.ds(pl.multiple_of(i * small, small), small)
            for r in range(NY):
                total += last[r:r + 1, :] * vr[r, rows, :].astype(jnp.float32)
            fin[rows, :] = total.astype(jnp.bfloat16)
            return carry

        lax.fori_loop(0, block_rows // small, final_rows, 0)
        for part, zs, yidx in ((part_a, az_sem, True), (part_b, bz_sem, False)):
            source = fin.at[pl.ds(*part)]
            goal = place(y, z, *part)
            for s in (1, -1):
                sem = az_sem.at[y, s % NZ] if yidx else bz_sem.at[s % NZ]
                size = lambda part=part: fin.at[pl.ds(*part)]
                send(source, goal, sem, dev(x, c, y, zn(s)), size=size)
                sem = ay_sem.at[0 if s > 0 else 1] if yidx else by_sem.at[0, 0 if s > 0 else 1]
                send(source, goal, sem, dev(x, c, yn(s), z), size=size)
        pltpu.make_async_copy(fin, place(y, z, 0, block_rows), load_sem.at[0]).start()

    mark = len(pending)
    pl.when(is_owner)(finish)
    pending[mark:] = [(ref, index, is_owner) for ref, index, _ in pending[mark:]]

    def z_forward(step, src_y, part, sems, cond):
        src = zn(-step)
        first, second = halves(part)
        if step in (1, 2):
            ref = place(src_y, src, *part)
            send(ref, ref, sems(step + 1), dev(x, c, y, zn(1)), cond)
        elif step in (-1, -2):
            ref = place(src_y, src, *part)
            send(ref, ref, sems((step - 1) % NZ), dev(x, c, y, zn(-1)), cond)
        elif step == 3:
            ref = place(src_y, src, *first)
            send(ref, ref, sems(4), dev(x, c, y, zn(1)), cond)
        elif step == -3:
            ref = place(src_y, src, *second)
            send(ref, ref, sems(0), dev(x, c, y, zn(-1)), cond)

    def z_arrived(step, src_y, part, sems):
        src = zn(-step)
        first, second = halves(part)
        if step == 4:
            arrived(place(src_y, src, *first), sems(4))
            arrived(place(src_y, src, *second), sems(0))
        else:
            arrived(place(src_y, src, *part), sems(step % NZ))

    def member(step):
        return zn(-step) // 4 == c

    def when(cond, task):
        pl.when(cond)(task)

    def ev_bz(step):
        cond = member(step)
        when(cond, lambda: z_arrived(step, y, part_b, lambda i: bz_sem.at[i]))
        z_forward(step, y, part_b, lambda i: bz_sem.at[i], cond)
        ref = place(y, zn(-step), *part_b)
        send(ref, ref, by_sem.at[step % NZ, 0], dev(x, c, yn(1), z), cond)
        send(ref, ref, by_sem.at[step % NZ, 1], dev(x, c, yn(-1), z), cond)

    def spread_y(sem, part, src_z, cond):
        first, second = halves(part)
        left, right = place(yn(-1), src_z, *part), place(yn(1), src_z, *part)
        when(cond, lambda: arrived(left, sem(0)))
        ref = place(yn(-1), src_z, *first)
        send(ref, ref, sem(2), dev(x, c, yn(1), z), cond)
        when(cond, lambda: arrived(right, sem(1)))
        ref = place(yn(1), src_z, *second)
        send(ref, ref, sem(3), dev(x, c, yn(-1), z), cond)

    def ev_by(step):
        spread_y(lambda i: by_sem.at[step % NZ, i], part_b, zn(-step), member(step))

    def ev_byend(step):
        first, second = halves(part_b)
        cond = member(step)
        when(cond, lambda: arrived(place(yn(2), zn(-step), *first), by_sem.at[step % NZ, 2]))
        when(cond, lambda: arrived(place(yn(2), zn(-step), *second), by_sem.at[step % NZ, 3]))

    def ev_ay():
        spread_y(lambda i: ay_sem.at[i], part_a, z, is_owner)
        for s in (1, -1):
            ref = place(yn(-s), z, *part_a)
            send(ref, ref, az_sem.at[yn(-s), 1], dev(x, c, y, zn(1)), is_owner)
            send(ref, ref, az_sem.at[yn(-s), NZ - 1], dev(x, c, y, zn(-1)), is_owner)

    def ev_ayend():
        first, second = halves(part_a)
        when(is_owner, lambda: arrived(place(yn(2), z, *first), ay_sem.at[2]))
        when(is_owner, lambda: arrived(place(yn(2), z, *second), ay_sem.at[3]))
        ref = place(yn(2), z, *part_a)
        send(ref, ref, az_sem.at[yn(2), 1], dev(x, c, y, zn(1)), is_owner)
        send(ref, ref, az_sem.at[yn(2), NZ - 1], dev(x, c, y, zn(-1)), is_owner)

    def ev_az(step, offset):
        cond = member(step)
        src_y = yn(offset)
        sems = lambda i: az_sem.at[src_y, i]
        when(cond, lambda: z_arrived(step, src_y, part_a, sems))
        z_forward(step, src_y, part_a, sems, cond)

    ev_ay()
    for step in (1, -1):
        ev_bz(step)
    ev_ayend()
    ev_by(0)
    for step in (1, -1):
        for offset in (0, 1, -1):
            ev_az(step, offset)
    for step in (2, -2):
        ev_bz(step)
    for step in (1, -1):
        ev_az(step, 2)
        ev_by(step)
    for step in (2, -2):
        for offset in (0, 1, -1):
            ev_az(step, offset)
    for step in (3, -3):
        ev_bz(step)
    for step in (2, -2):
        ev_az(step, 2)
        ev_by(step)
    for step in (3, -3):
        for offset in (0, 1, -1, 2):
            ev_az(step, offset)
        ev_by(step)
    ev_bz(4)
    for offset in (0, 1, -1, 2):
        ev_az(4, offset)
    ev_by(4)
    for step in (0, 1, -1, 2, -2, 3, -3, 4):
        ev_byend(step)
    drain(pending)
    pl.when(is_owner)(
        pltpu.make_async_copy(fin, place(y, z, 0, block_rows), load_sem.at[0]).wait
    )


def on_device(tokens, pre_act, act_grad):
    tok, feat = tokens.shape
    width = pre_act.shape[1]
    feats, cols = feat // 2, width // 2
    rows = feats * NX
    bf16, f32 = jnp.bfloat16, jnp.float32
    dma = pltpu.SemaphoreType.DMA
    return pl.pallas_call(
        kernel,
        out_shape=jax.ShapeDtypeStruct((feat * 2 * NX, width), bf16),
        in_specs=[
            pl.BlockSpec(memory_space=pltpu.VMEM),
            pl.BlockSpec(memory_space=pl.ANY),
            pl.BlockSpec(memory_space=pl.ANY),
        ],
        out_specs=pl.BlockSpec(memory_space=pl.ANY),
        scratch_shapes=[
            pltpu.VMEM((NZ, NX, feats, tok), bf16),
            pltpu.VMEM((NZ, tok, cols), bf16),
            pltpu.VMEM((2, tok, cols), bf16),
            pltpu.VMEM((tok, width), bf16),
            pltpu.VMEM((tok, width), bf16),
            pltpu.VMEM((NZ, rows, cols), bf16),
            pltpu.VMEM((256, 256), f32),
            pltpu.VMEM((NY, feats, cols), bf16),
            pltpu.VMEM((NY, 2 * feats, cols), bf16),
            pltpu.VMEM((2 * feats, cols), bf16),
            pltpu.VMEM((2 * NX, 8, 128), f32),
            pltpu.VMEM((NZ, 8, 128), f32),
            pltpu.VMEM((NX * NY, 8, 128), f32),
            pltpu.VMEM((NZ, 8, 128), f32),
            dma((2,)),
            dma((SEND_SEMS,)),
            dma((NZ,)),
            dma((NZ, 4)),
            dma((NZ,)),
            dma((NZ,)),
            dma((NY, 2)),
            dma((4,)),
            dma((NZ,)),
            dma((NZ, 4)),
            dma((NY, NZ)),
            dma((4,)),
        ],
        compiler_params=pltpu.CompilerParams(
            collective_id=0, has_side_effects=True, vmem_limit_bytes=48 * 1024 * 1024
        ),
    )(tokens.T, pre_act, act_grad)


def solution(mesh):
    return jax.shard_map(
        on_device,
        mesh=mesh,
        in_specs=(P("dp", "tp"), P("dp", "tp"), P("dp", "tp")),
        out_specs=P(None, "tp"),
        check_vma=False,
    )
```

time: 844 us -> 180 us (0.21)
  blocking collectives: 373 us -> 0 us
  waiting for transfers between devices: 373 us -> 0 us
  Pallas kernels: 0 us -> 170 us
  other arithmetic: 39.5 us -> 0 us
  between operations: 25.9 us -> 0.01 us
  starting transfers between devices: 9.38 us -> 0 us
    psum x5 -> x0, blocking collectives: 373 us -> none  [on_device(): summed = lax.psum(table, ('dp', 'tp'))]
    ppermute x5 -> x0, waiting for transfers between devices: 252 us -> none  [swapped(): return lax.ppermute(block, axis, route)]
    pallas_call x0 -> x1, Pallas kernels: none -> 170 us  [on_device(): pl.pallas_call(kernel, out_shape=jax.ShapeDtypeStruct((feat * 2 * NX, wid...]
    all_gather x2 -> x0, waiting for transfers between devices: 120 us -> none  [the longest x1 85.5 us: on_device(): combined = lax.all_gather(holding, 'dp', axis=0, tiled=True)]
    reduce_sum x9 -> x0, other arithmetic: 18.2 us -> none  [the longest x5 17.8 us: on_device(): jnp.sum(lower_part * upper_part)]
    another operation x5 -> x0, other arithmetic: 9.59 us -> none  [on_device(): jnp.stack([jnp.sum(lower_part * upper_part), jnp.sum(lower_part * lower_p...]
    ppermute x5 -> x0, starting transfers between devices: 9.34 us -> none  [swapped(): return lax.ppermute(block, axis, route)]
    convert_element_type x9 -> x0, other arithmetic: 8.97 us -> none  [the longest x5 8.95 us: on_device(): (lower_coef * lower_part + upper_coef * upper_part).astype(jnp.bfloat16)]
  transfers between devices with their start and end apart: 7 -> 0, of which waited for: 7 -> 0; matrix products, arithmetic and copies ran while one was open for 0% -> 0% of each run, Pallas kernels for 0% -> 0%
where the time goes in v1:
time: 180 us; the launch traced here: 179 us
  Pallas kernels  170 us (94%)
  local copies, waits for them, and re-layouts  9.67 us (5%)
    pallas_call x1, Pallas kernels, on_device(): pl.pallas_call(kernel, out_shape=jax.ShapeDtypeStruct((feat * 2 * NX, wid...  170 us
    unnamed x7, local copies, waits for them, and re-layouts  9.67 us

profile of v1, /device:TPU:1, one launch (start us, length us, event | category | flops | bytes accessed | tf_op | source)
XLA Modules:
  0.0 179.4 jit_solution(13529424649339885108)
XLA Ops:
  0.0 0.0 copy-start
  0.0 1.3 copy-done
  1.3 0.0 copy-start.1
  1.3 1.3 copy-done.1
  2.6 0.0 copy-start.2
  2.6 1.0 copy-done.2
  3.6 169.8 %shard_map.37 = bf16[2560,1280]{1,0:T(8,128)(2,1)} custom-call(bf16[320,512]{1,0:T(8,128)(2,1)S(1)} %bitcast.1, bf16[512,1280]{1,0:T(8,128)(2,1)S(1)} %copy-done, bf16[512,1280]{1,0:T(8,128)(2,1)S(1)} %copy-done.1), custom_call_target="tpu_custom_call" | custom-call | tf_op jit(solution)/shard_map/pallas_call | solution.py:480
  173.4 6.1 %copy.5 = bf16[2560,1280]{1,0:T(8,128)(2,1)} copy(bf16[2560,1280]{1,0:T(8,128)(2,1)} %shard_map.37) | data formatting | bytes 13107200
Async XLA Ops:
  0.0 1.3 copy-start
  1.3 1.3 copy-start.1
  2.6 1.0 copy-start.2

commit v2 on v1

--- a/solution.py
+++ b/solution.py
@@ -48,30 +48,39 @@
     return weight
 
 
-def fold_gram(product, count, group):
-    size = count * group
-    row = lax.broadcasted_iota(jnp.int32, (size, size), 0)
-    lane = lax.broadcasted_iota(jnp.int32, (size, size), 1)
-    kept = jnp.where(row % group == lane % group, product, 0.0)
-    rows = jnp.sum(kept.reshape(count, group, size), axis=1)
-    lane = lax.broadcasted_iota(jnp.int32, (count, size), 1)
-    out_lane = lax.broadcasted_iota(jnp.int32, (count, 128), 1)
-    total = jnp.zeros((count, 128), jnp.float32)
-    for index in range(count):
-        one = jnp.sum(jnp.where(lane // group == index, rows, 0.0), axis=1, keepdims=True)
-        total = jnp.where(out_lane % count == index, one, total)
-    return total
+def lane_sums(values):
+    total = values[:, :128]
+    for start in range(128, values.shape[1], 128):
+        total = total + values[:, start:start + 128]
+    return total[:8] + total[8:]
+
+
+def exact_dot(left, right):
+    return jnp.dot(
+        left, right, preferred_element_type=jnp.float32, precision=lax.Precision.HIGHEST
+    )
+
+
+def fold(sums):
+    size = sums.shape[0] * sums.shape[1] * sums.shape[2]
+    across = exact_dot(sums.reshape(size, 128), jnp.ones((128, 128), jnp.float32))
+    row = lax.broadcasted_iota(jnp.int32, (size, 128), 0)
+    lane = lax.broadcasted_iota(jnp.int32, (size, 128), 1)
+    kept = jnp.where(row // 8 % 8 == lane % 8, across, 0.0)
+    return jnp.sum(kept.reshape(8, size // 8, 128), axis=1)
 
 
 def kernel(
     xt, pre, act, out,
-    xb, yb, ys, pre_v, act_v, grads, prod, vs, vr, fin,
+    xb, yb, ys, pre_v, act_v, grads, pairs, vs, vr, fin,
     a1, a2, b1, b2,
     load_sem, send_sem, xz_sem, xx_sem, yz_sem, yy_sem, v_sem, ar_sem,
     bz_sem, by_sem, az_sem, ay_sem,
 ):
     dp, tp = lax.axis_index("dp"), lax.axis_index("tp")
     z, y, x, c = dp // NY, dp % NY, tp // 2, tp % 2
+    toward = 1 - 2 * (z % 2)
+    kind = (z + 1) // 2 % 2
     tokens = yb.shape[1]
     half_tok = tokens // 2
     feats = xb.shape[2]
@@ -82,6 +91,9 @@
 
     def zn(step):
         return (z + step + NZ) % NZ
+
+    def zt(step):
+        return zn(step * toward)
 
     def yn(step):
         return (y + step + NY) % NY
@@ -131,69 +143,69 @@
         pl.semaphore_signal(barrier, inc=1, device_id=partner, device_id_type=MESH)
     pl.semaphore_wait(barrier, len(partners))
 
-    match = z % 2 == c
-    reach = jnp.where(match, 2, 1)
-    for sign in (1, -1):
+    match = kind == c
+    for near, far in ((-1, 3), (1, -2)):
+        cond = match if near < 0 else jnp.logical_not(match)
         for k in range(2):
-            send(
-                xt.at[pl.ds(k * feats, feats)], xb.at[z, x], xz_sem.at[z],
-                dev(x, k, y, (z + sign * reach + NZ) % NZ),
-            )
+            rows = xt.at[pl.ds(k * feats, feats)]
+            send(rows, xb.at[z, x], xz_sem.at[z], dev(x, k, y, zt(far)), cond)
+            send(rows, xb.at[z, x], xz_sem.at[z], dev(x, k, y, zt(near)), cond)
     other = pl.multiple_of((1 - c) * feats, 16)
     mine = pl.multiple_of(c * feats, 16)
     own_x = pltpu.make_async_copy(xt.at[pl.ds(mine, feats)], xb.at[z, x], xz_sem.at[z])
     pl.when(match)(own_x.start)
     send(xt.at[pl.ds(other, feats)], xb.at[z, x], xz_sem.at[z], dev(x, 1 - c, y, z), match)
 
-    for load in loads:
-        load.wait()
     chunk = 32
     my_pair, my_parity = z // 2, z % 2
-    for j in range(2):
+    first = jnp.where((c - my_pair + 4) % 4 == 0, 1, 0)
+
+    def ev_sl(turn):
+        if turn == 0:
+            for load in loads:
+                load.wait()
+        j = first if turn == 0 else 1 - first
+        span = pl.ds(pl.multiple_of(j * cols, 128), cols)
+
         def slope_rows(i, carry):
             rows = pl.ds(pl.multiple_of(i * chunk, chunk), chunk)
-            span = pl.ds(j * cols, cols)
             slope = gelu_slope(pre_v[rows, span].astype(jnp.float32))
-            ys[j, rows, :] = (act_v[rows, span].astype(jnp.float32) * slope).astype(jnp.bfloat16)
+            ys[turn, rows, :] = (act_v[rows, span].astype(jnp.float32) * slope).astype(jnp.bfloat16)
             return carry
 
         lax.fori_loop(0, tokens // chunk, slope_rows, 0)
-        quarter = 2 * c + j
-        ahead = (quarter - my_pair + 4) % 4
+
+    def ev_ys(turn):
+        pair = c + 2 * (first if turn == 0 else 1 - first)
+        ahead = (pair - my_pair + 4) % 4
         upper = jnp.where(
             ahead == 0, 1 - my_parity,
             jnp.where(ahead == 3, 1, jnp.where(ahead == 2, 1 - my_parity, 0)),
         )
-        target = 2 * quarter + upper
+        target = 2 * pair + upper
         for k in range(2):
             rows = pl.ds(k * half_tok, half_tok)
-            send(ys.at[j, rows], yb.at[z, rows], yz_sem.at[z], dev(x, k, y, target))
+            send(ys.at[turn, rows], yb.at[z, rows], yz_sem.at[z], dev(x, k, y, target))
         own = ahead == 0
         own_rows = pl.ds(pl.multiple_of(c * half_tok, 16), half_tok)
         other_rows = pl.ds(pl.multiple_of((1 - c) * half_tok, 16), half_tok)
-        own_y = pltpu.make_async_copy(ys.at[j, own_rows], yb.at[z, own_rows], yz_sem.at[z])
+        own_y = pltpu.make_async_copy(ys.at[turn, own_rows], yb.at[z, own_rows], yz_sem.at[z])
         pl.when(own)(own_y.start)
-        send(ys.at[j, other_rows], yb.at[z, other_rows], yz_sem.at[z], dev(x, 1 - c, y, z), own)
+        send(ys.at[turn, other_rows], yb.at[z, other_rows], yz_sem.at[z], dev(x, 1 - c, y, z), own)
 
     def ev_xz(step):
-        src = zn(-step)
+        src = zt(step)
         piece = xb.at[src, x]
         arrived(piece, xz_sem.at[src])
-        if step == 1:
-            send(piece, piece, xz_sem.at[src], dev(x, c, y, zn(2)))
-        if step == -1:
-            send(piece, piece, xz_sem.at[src], dev(x, c, y, zn(-2)))
-        if step == 2:
-            send(piece, piece, xz_sem.at[src], dev(x, c, y, zn(2)), c == 0)
-        if step == -2:
-            send(piece, piece, xz_sem.at[src], dev(x, c, y, zn(-2)), c == 1)
+        if step in (1, 2, 3):
+            send(piece, piece, xz_sem.at[src], dev(x, c, y, zt(-1)))
         send(piece, piece, xx_sem.at[src, 0], dev(xn(1), c, y, z))
         send(piece, piece, xx_sem.at[src, 1], dev(xn(-1), c, y, z))
 
     low, high = pl.ds(0, feats // 2), pl.ds(feats // 2, feats // 2)
 
     def ev_xx(step):
-        src = zn(-step)
+        src = zt(step)
         left, right = xb.at[src, xn(-1)], xb.at[src, xn(1)]
         arrived(left, xx_sem.at[src, 0])
         send(left.at[low], left.at[low], xx_sem.at[src, 2], dev(xn(1), c, y, z))
@@ -204,17 +216,15 @@
     its_tok = pl.ds(pl.multiple_of((1 - c) * half_tok, 16), half_tok)
 
     def ev_yz(step):
-        src = zn(-step)
+        src = zt(step)
         piece = yb.at[src, my_tok]
         arrived(piece, yz_sem.at[src])
-        if step in (1, 2, 3):
-            send(piece, piece, yz_sem.at[src], dev(x, c, y, zn(1)), z % 2 == 0)
         if step in (-1, -2, -3):
-            send(piece, piece, yz_sem.at[src], dev(x, c, y, zn(-1)), z % 2 == 1)
+            send(piece, piece, yz_sem.at[src], dev(x, c, y, zt(1)))
         send(piece, piece, yy_sem.at[src], dev(x, 1 - c, y, z))
 
     def ev_mm(step):
-        src = zn(-step)
+        src = zt(step)
         far = xb.at[src, xn(2)]
         arrived(far.at[low], xx_sem.at[src, 2])
         arrived(far.at[high], xx_sem.at[src, 3])
@@ -226,30 +236,36 @@
             return carry
 
         lax.fori_loop(0, NX, block, 0)
-
+        done.append(src)
+
+        def products(i, sums):
+            rows = pl.ds(pl.multiple_of(i * 16, 16), 16)
+            new = grads[src, rows, :].astype(jnp.float32)
+            return tuple(
+                total + lane_sums(new * (new if old is src else grads[old, rows, :].astype(jnp.float32)))
+                for old, total in zip(done, sums)
+            )
+
+        zero = jnp.zeros((8, 128), jnp.float32)
+        sums = lax.fori_loop(0, grads.shape[1] // 16, products, (zero,) * len(done))
+        for old, total in zip(done, sums):
+            pairs[src, old] = total
+            if old is not src:
+                pairs[old, src] = total
+
+    done = []
     xz, xx, yz, mm = ev_xz, ev_xx, ev_yz, ev_mm
+    sl, yt = ev_sl, ev_ys
     for event, step in [
-        (xz, 0), (xz, 1), (xz, -1), (xx, 0), (xz, 2), (xz, -2), (xx, 1), (xx, -1),
-        (yz, 0), (yz, 1), (yz, -1), (xx, 2), (xx, -2), (xz, 3), (xz, -3), (xz, 4), (mm, 0),
-        (yz, 2), (yz, -2), (xx, 3), (xx, -3), (mm, 1), (mm, -1), (yz, 3), (yz, -3), (xx, 4),
-        (mm, 2), (mm, -2), (yz, 4), (mm, 3), (mm, -3), (mm, 4),
+        (xz, 0), (sl, 0), (xz, -1), (xz, 1), (sl, 1), (xx, 0), (xz, 2), (xz, 3), (yt, 0), (yt, 1),
+        (xx, -1), (xx, 1), (xz, -2), (xz, -3), (xx, 2), (xz, 4), (yz, 0), (yz, 1), (yz, -1), (xx, 3), (xx, -2), (xx, -3),
+        (mm, 0), (yz, -2), (xx, 4), (mm, 1), (yz, -3), (mm, -1), (yz, 2), (mm, -2), (yz, 3),
+        (mm, 2), (mm, -3), (yz, 4), (mm, 3), (mm, 4),
     ]:
         event(step)
 
-    group = 32
-    total_rows = grads.shape[1]
-    prod[...] = jnp.zeros_like(prod)
-
-    def gram_rows(i, carry):
-        rows = pl.ds(pl.multiple_of(i * group, group), group)
-        stacked = grads[:, rows, :].reshape(NZ * group, cols)
-        prod[...] += lax.dot_general(
-            stacked, stacked, (((1,), (1,)), ((), ())), preferred_element_type=jnp.float32
-        )
-        return carry
-
-    lax.fori_loop(0, total_rows // group, gram_rows, 0)
-    a1[tp] = fold_gram(prod[...], NZ, group)
+    out_lane = lax.broadcasted_iota(jnp.int32, (8, 128), 1)
+    a1[tp] = fold(pairs[...])
     for s in range(1, 2 * NX):
         send(a1.at[tp], a1.at[tp], ar_sem.at[0], (dp, (tp + s) % (2 * NX)))
     sent = pl.ds(0, 2 * NX - 1)
@@ -257,12 +273,10 @@
     a2[z] = jnp.sum(a1[...], axis=0)
     for s in range(1, NZ):
         send(a2.at[z], a2.at[z], ar_sem.at[1], dev(x, c, y, zn(s)))
-    drain(pending)
-    pending.clear()
     arrived(a2.at[pl.ds(0, NZ - 1)], ar_sem.at[1])
     weight = tree_weights(jnp.sum(a2[...], axis=0), (4, 2, 1))
 
-    owner = z // 4
+    owner = z // 2 % 2
     is_owner = c == owner
     its_rows = pl.ds(pl.multiple_of(c * feats, 16), feats)
     small = 32
@@ -291,8 +305,8 @@
     part_a, part_b = (0, cut), (cut, block_rows - cut)
 
     def place(y_, z_, start, size):
-        top = pl.multiple_of((2 * y_ + z_ % 2) * block_rows + start, 16)
-        left = pl.multiple_of((z_ // 2) % 2 * cols, 128)
+        top = pl.multiple_of((2 * y_ + (z_ + 1) // 2 % 2) * block_rows + start, 16)
+        left = pl.multiple_of(z_ // 4 * cols, 128)
         return out.at[pl.ds(top, size), pl.ds(left, cols)]
 
     def halves(part):
@@ -303,21 +317,25 @@
         for src in range(NY):
             for k in range(2):
                 arrived(vr.at[src, pl.ds(k * feats, feats)], v_sem.at[src, k])
-        size = NY * group
-        prod[0:size, 0:size] = jnp.zeros((size, size), jnp.float32)
-
-        def gram(i, carry):
-            rows = pl.ds(pl.multiple_of(i * group, group), group)
-            stacked = vr[:, rows, :].reshape(size, cols)
-            prod[0:size, 0:size] += lax.dot_general(
-                stacked, stacked, (((1,), (1,)), ((), ())), preferred_element_type=jnp.float32
+        def products(i, sums):
+            rows = pl.ds(pl.multiple_of(i * 16, 16), 16)
+            parts = [vr[r, rows, :].astype(jnp.float32) for r in range(NY)]
+            return tuple(
+                total + lane_sums(parts[a] * parts[b]) for (a, b), total in zip(combos, sums)
             )
-            return carry
-
-        lax.fori_loop(0, block_rows // group, gram, 0)
-        folded = fold_gram(prod[0:size, 0:size], NY, group)
+
+        combos = [(a, b) for a in range(NY) for b in range(a, NY)]
+        zero = jnp.zeros((8, 128), jnp.float32)
+        sums = lax.fori_loop(0, block_rows // 16, products, (zero,) * len(combos))
+        out_row = lax.broadcasted_iota(jnp.int32, (8, 128), 0) % NY
+        out_col = out_lane % NY
+        gram = zero
+        for (a, b), total in zip(combos, sums):
+            value = jnp.sum(total, axis=(0, 1), keepdims=True)
+            spot = ((out_row == a) & (out_col == b)) | ((out_row == b) & (out_col == a))
+            gram = jnp.where(spot, value, gram)
         me = x * NY + y
-        b1[me] = jnp.concatenate([folded, folded], axis=0)
+        b1[me] = gram
         for s in range(NX):
             for t in range(NY):
                 if s or t:
@@ -325,7 +343,7 @@
         arrived(b1.at[pl.ds(0, NX * NY - 1)], ar_sem.at[2])
         b2[z] = jnp.sum(b1[...], axis=0)
         for s in range(1, NZ):
-            send(b2.at[z], b2.at[z], ar_sem.at[3], dev(x, zn(s) // 4, y, zn(s)), size=lambda: b2.at[0])
+            send(b2.at[z], b2.at[z], ar_sem.at[3], dev(x, zn(s) // 2 % 2, y, zn(s)), size=lambda: b2.at[0])
         arrived(b2.at[pl.ds(0, NZ - 1)], ar_sem.at[3])
         last = tree_weights(jnp.sum(b2[...], axis=0), (2, 1))
 
@@ -338,15 +356,16 @@
             return carry
 
         lax.fori_loop(0, block_rows // small, final_rows, 0)
-        for part, zs, yidx in ((part_a, az_sem, True), (part_b, bz_sem, False)):
-            source = fin.at[pl.ds(*part)]
-            goal = place(y, z, *part)
-            for s in (1, -1):
-                sem = az_sem.at[y, s % NZ] if yidx else bz_sem.at[s % NZ]
-                size = lambda part=part: fin.at[pl.ds(*part)]
-                send(source, goal, sem, dev(x, c, y, zn(s)), size=size)
-                sem = ay_sem.at[0 if s > 0 else 1] if yidx else by_sem.at[0, 0 if s > 0 else 1]
-                send(source, goal, sem, dev(x, c, yn(s), z), size=size)
+        def launch(part, sem, device):
+            send(fin.at[pl.ds(*part)], place(y, z, *part), sem, device,
+                 size=lambda: fin.at[pl.ds(*part)])
+
+        for s in (1, -1):
+            launch(part_b, bz_sem.at[s % NZ], dev(x, c, y, zn(s)))
+            launch(part_a, ay_sem.at[0 if s > 0 else 1], dev(x, c, yn(s), z))
+        for s in (1, -1):
+            launch(part_b, by_sem.at[0, 0 if s > 0 else 1], dev(x, c, yn(s), z))
+            launch(part_a, az_sem.at[y, s % NZ], dev(x, c, y, zn(s)))
         pltpu.make_async_copy(fin, place(y, z, 0, block_rows), load_sem.at[0]).start()
 
     mark = len(pending)
@@ -379,7 +398,7 @@
             arrived(place(src_y, src, *part), sems(step % NZ))
 
     def member(step):
-        return zn(-step) // 4 == c
+        return zn(-step) // 2 % 2 == c
 
     def when(cond, task):
         pl.when(cond)(task)
@@ -479,13 +498,13 @@
     dma = pltpu.SemaphoreType.DMA
     return pl.pallas_call(
         kernel,
-        out_shape=jax.ShapeDtypeStruct((feat * 2 * NX, width), bf16),
+        out_shape=pltpu.VMEM((feat * 2 * NX, width), bf16),
         in_specs=[
-            pl.BlockSpec(memory_space=pltpu.VMEM),
+            pl.BlockSpec(memory_space=pl.ANY),
             pl.BlockSpec(memory_space=pl.ANY),
             pl.BlockSpec(memory_space=pl.ANY),
         ],
-        out_specs=pl.BlockSpec(memory_space=pl.ANY),
+        out_specs=pl.BlockSpec(memory_space=pltpu.VMEM),
         scratch_shapes=[
             pltpu.VMEM((NZ, NX, feats, tok), bf16),
             pltpu.VMEM((NZ, tok, cols), bf16),
@@ -493,7 +512,7 @@
             pltpu.VMEM((tok, width), bf16),
             pltpu.VMEM((tok, width), bf16),
             pltpu.VMEM((NZ, rows, cols), bf16),
-            pltpu.VMEM((256, 256), f32),
+            pltpu.VMEM((NZ, NZ, 8, 128), f32),
             pltpu.VMEM((NY, feats, cols), bf16),
             pltpu.VMEM((NY, 2 * feats, cols), bf16),
             pltpu.VMEM((2 * feats, cols), bf16),
@@ -515,7 +534,7 @@
             dma((4,)),
         ],
         compiler_params=pltpu.CompilerParams(
-            collective_id=0, has_side_effects=True, vmem_limit_bytes=48 * 1024 * 1024
+            collective_id=0, has_side_effects=True, vmem_limit_bytes=52 * 1024 * 1024
         ),
     )(tokens.T, pre_act, act_grad)
 

time: 180 us -> 174 us (0.967)
  the two profiles are of different devices: /device:TPU:1 before, /device:TPU:32 now
where the time goes in v2:
time: 174 us
  Pallas kernels  172 us (99%)
  local copies, waits for them, and re-layouts  2.79 us (2%)
    pallas_call x1, Pallas kernels, on_device(): pl.pallas_call(kernel, out_shape=pltpu.VMEM((feat * 2 * NX, width), bf16)...  172 us

profile of v2, /device:TPU:32, one launch (start us, length us, event | category | flops | bytes accessed | tf_op | source)
XLA Modules:
  0.0 174.4 jit_solution(836797266930806294)
XLA Ops:
  0.0 171.6 %shard_map.37 = bf16[2560,1280]{1,0:T(8,128)(2,1)S(1)} custom-call(bf16[320,512]{1,0:T(8,128)(2,1)} %bitcast.1, bf16[512,1280]{1,0:T(8,128)(2,1)} %pre.1, bf16[512,1280]{1,0:T(8,128)(2,1)} %act.1), custom_call_target="tpu_custom_call" | custom-call | tf_op jit(solution)/shard_map/pallas_call | solution.py:499
  171.6 2.8 %copy.5 = bf16[2560,1280]{1,0:T(8,128)(2,1)} copy(bf16[2560,1280]{1,0:T(8,128)(2,1)S(1)} %shard_map.37) | data formatting | bytes 13107200

commit v3 on v2

v3 whole, which is shorter than its diff:
```python
import jax
import jax.numpy as jnp
from jax import lax
from jax.experimental import pallas as pl
from jax.experimental.pallas import tpu as pltpu
from jax.sharding import PartitionSpec as P

norm_epsilon = 1e-06
gelu_scale = 0.7978845608
MESH = pl.DeviceIdType.MESH
NX, NY, NZ = 4, 4, 8
SEND_SEMS = 80

OWNER_EVENTS = [
    ("source_y",), ("source_z",), ("first_z", 0), ("turn_y", 0), ("pass_y",), ("first_z", -1),
    ("b_along_z", -1), ("turn_y", -1), ("last_y",), ("first_z", 2), ("first_z", 1), ("b_along_y", 0),
    ("a_along_z", -1, 2), ("b_along_y", -1), ("a_along_z", -1, 0), ("a_along_z", -1, 1), ("b_along_z", 3),
    ("a_along_z", -1, -1), ("turn_y", 3), ("b_along_z", 4), ("b_end", -1), ("b_end", 0), ("turn_y", 4),
    ("a_along_z", 3, -1), ("a_along_z", 3, 2), ("b_along_y", 3), ("b_along_y", 4), ("a_along_z", 4, 0),
    ("a_along_z", 4, 1), ("a_along_z", 3, 1), ("a_along_z", 4, 2), ("b_end", 3), ("a_along_z", 3, 0),
    ("a_along_z", 4, -1), ("b_end", 4),
]
OTHER_EVENTS = [
    ("b_along_z", 1), ("turn_y", 1), ("b_along_z", -2), ("turn_y", -2), ("b_along_z", 2), ("turn_y", 2),
    ("a_along_z", 1, 2), ("a_along_z", 1, 1), ("a_along_z", 1, -1), ("a_along_z", 1, 0), ("a_along_z", 2, 0),
    ("b_along_z", -3), ("b_along_y", 1), ("turn_y", -3), ("a_along_z", -2, 1), ("a_along_z", -2, 2),
    ("b_along_y", 2), ("a_along_z", 2, -1), ("a_along_z", 2, 1), ("a_along_z", -2, -1), ("b_end", 1),
    ("a_along_z", 2, 2), ("a_along_z", -3, 0), ("b_along_y", -2), ("b_along_y", -3), ("a_along_z", -3, -1),
    ("a_along_z", -2, 0), ("a_along_z", -3, 1), ("a_along_z", -3, 2), ("b_end", 2), ("b_end", -3),
    ("b_end", -2),
]


def gelu_slope(values):
    inner = gelu_scale * (values + 0.044715 * values * values * values)
    tangent = jnp.tanh(inner)
    return 0.5 * (1.0 + tangent) + 0.5 * values * (1.0 - tangent * tangent) * gelu_scale * (
        1.0 + 0.134145 * values * values
    )


def tree_weights(gram, strides):
    shape = gram.shape
    row = lax.broadcasted_iota(jnp.int32, shape, 0)
    lane = lax.broadcasted_iota(jnp.int32, shape, 1)
    own = lane % 8 == row
    first = lane < 8
    weight = jnp.ones((8, 1), jnp.float32)
    for stride in strides:
        pair = lane % 8 == (row + stride) % 8
        own_col = jnp.sum(jnp.where(own & first, gram, 0.0), axis=1, keepdims=True)
        pair_col = jnp.sum(jnp.where(pair & first, gram, 0.0), axis=1, keepdims=True)
        own_row = jnp.sum(jnp.where(own, gram, 0.0), axis=0, keepdims=True)
        pair_row = jnp.sum(
            jnp.where(row == (lane + stride) % 8, gram, 0.0), axis=0, keepdims=True
        )
        coef_col = 1.0 - pair_col / (2.0 * (jnp.maximum(own_col, 0.0) + norm_epsilon))
        coef_row = 1.0 - pair_row / (2.0 * (jnp.maximum(own_row, 0.0) + norm_epsilon))
        weight = weight * coef_col
        scaled = gram * coef_col * coef_row
        scaled = scaled + pltpu.roll(scaled, stride, 0)
        gram = scaled + pltpu.roll(scaled, stride, 1)
    return weight


def lane_sums(values):
    total = values[:, :128]
    for start in range(128, values.shape[1], 128):
        total = total + values[:, start:start + 128]
    return total[:8] + total[8:]


def exact_dot(left, right):
    return jnp.dot(
        left, right, preferred_element_type=jnp.float32, precision=lax.Precision.HIGHEST
    )


def fold(sums):
    size = sums.shape[0] * sums.shape[1] * sums.shape[2]
    across = exact_dot(sums.reshape(size, 128), jnp.ones((128, 128), jnp.float32))
    row = lax.broadcasted_iota(jnp.int32, (size, 128), 0)
    lane = lax.broadcasted_iota(jnp.int32, (size, 128), 1)
    kept = jnp.where(row // 8 % 8 == lane % 8, across, 0.0)
    return jnp.sum(kept.reshape(8, size // 8, 128), axis=1)


def kernel(
    xt, pre, act, out,
    xb, yb, ys, pre_v, act_v, grads, pairs, vs, vr,
    a1, a2, b1, b2,
    load_sem, send_sem, group_sem, xz_sem, xx_sem, yz_sem, yy_sem, v_sem, ar_sem,
    bz_sem, by_sem, az_sem, ay_sem,
):
    dp, tp = lax.axis_index("dp"), lax.axis_index("tp")
    z, y, x, c = dp // NY, dp % NY, tp // 2, tp % 2
    toward = 1 - 2 * (z % 2)
    kind = (z + 1) // 2 % 2
    tokens = yb.shape[1]
    half_tok = tokens // 2
    feats = xb.shape[2]
    cols = yb.shape[2]

    def dev(x_, c_, y_, z_):
        return (z_ * NY + y_, x_ * 2 + c_)

    def zn(step):
        return (z + step + NZ) % NZ

    def zt(step):
        return zn(step * toward)

    def yn(step):
        return (y + step + NY) % NY

    def xn(step):
        return (x + step + NX) % NX

    pending = []
    counter = [0]

    def send(src, dst, recv, device, cond=None, group=None, waits=pending):
        if group is None:
            sent = send_sem.at[counter[0]]
            waits.append((src, counter[0], cond))
            counter[0] += 1
        else:
            sent = group_sem.at[group]
        copy = pltpu.make_async_remote_copy(
            src_ref=src, dst_ref=dst, send_sem=sent, recv_sem=recv,
            device_id=device, device_id_type=MESH,
        )
        if cond is None:
            copy.start()
        else:
            pl.when(cond)(copy.start)

    def arrived(ref, sem):
        pltpu.make_async_copy(ref, ref, sem).wait()

    def drain(items):
        for ref, index, cond in items:
            if cond is None:
                arrived(ref, send_sem.at[index])
            else:
                pl.when(cond)(lambda: arrived(ref, send_sem.at[index]))

    loads = [
        pltpu.make_async_copy(pre, pre_v, load_sem.at[0]),
        pltpu.make_async_copy(act, act_v, load_sem.at[1]),
    ]
    for load in loads:
        load.start()

    barrier = pltpu.get_barrier_semaphore()
    partners = [dev(x, k, y, zn(s)) for s in range(1, NZ) for k in range(2)]
    partners += [dev(x, 1 - c, y, z)]
    partners += [dev(xn(s), k, y, z) for s in range(1, NX) for k in range(2)]
    partners += [dev(x, k, yn(s), z) for s in range(1, NY) for k in range(2)]
    partners += [dev(xn(s), c, yn(t), z) for s in range(1, NX) for t in range(1, NY)]
    for partner in partners:
        pl.semaphore_signal(barrier, inc=1, device_id=partner, device_id_type=MESH)
    pl.semaphore_wait(barrier, len(partners))

    match = kind == c
    for near, far in ((-1, 3), (1, -2)):
        cond = match if near < 0 else jnp.logical_not(match)
        for k in range(2):
            rows = xt.at[pl.ds(k * feats, feats)]
            send(rows, xb.at[z, x], xz_sem.at[z], dev(x, k, y, zt(far)), cond, group=0)
            send(rows, xb.at[z, x], xz_sem.at[z], dev(x, k, y, zt(near)), cond, group=0)
    other = pl.multiple_of((1 - c) * feats, 16)
    mine = pl.multiple_of(c * feats, 16)
    own_x = pltpu.make_async_copy(xt.at[pl.ds(mine, feats)], xb.at[z, x], xz_sem.at[z])
    pl.when(match)(own_x.start)
    send(xt.at[pl.ds(other, feats)], xb.at[z, x], xz_sem.at[z], dev(x, 1 - c, y, z), match)

    chunk = 32
    my_pair, my_parity = z // 2, z % 2
    first = jnp.where((c - my_pair + 4) % 4 == 0, 1, 0)

    def ev_sl(turn):
        if turn == 0:
            for load in loads:
                load.wait()
        j = first if turn == 0 else 1 - first
        span = pl.ds(pl.multiple_of(j * cols, 128), cols)

        def slope_rows(i, carry):
            rows = pl.ds(pl.multiple_of(i * chunk, chunk), chunk)
            slope = gelu_slope(pre_v[rows, span].astype(jnp.float32))
            ys[turn, rows, :] = (act_v[rows, span].astype(jnp.float32) * slope).astype(jnp.bfloat16)
            return carry

        lax.fori_loop(0, tokens // chunk, slope_rows, 0)

    def ev_ys(turn):
        pair = c + 2 * (first if turn == 0 else 1 - first)
        ahead = (pair - my_pair + 4) % 4
        upper = jnp.where(
            ahead == 0, 1 - my_parity,
            jnp.where(ahead == 3, 1, jnp.where(ahead == 2, 1 - my_parity, 0)),
        )
        target = 2 * pair + upper
        for k in range(2):
            rows = pl.ds(k * half_tok, half_tok)
            send(ys.at[turn, rows], yb.at[z, rows], yz_sem.at[z], dev(x, k, y, target), group=2)
        own = ahead == 0
        own_rows = pl.ds(pl.multiple_of(c * half_tok, 16), half_tok)
        other_rows = pl.ds(pl.multiple_of((1 - c) * half_tok, 16), half_tok)
        own_y = pltpu.make_async_copy(ys.at[turn, own_rows], yb.at[z, own_rows], yz_sem.at[z])
        pl.when(own)(own_y.start)
        send(ys.at[turn, other_rows], yb.at[z, other_rows], yz_sem.at[z], dev(x, 1 - c, y, z), own)

    def ev_xz(step):
        src = zt(step)
        piece = xb.at[src, x]
        arrived(piece, xz_sem.at[src])
        if step in (1, 2, 3):
            send(piece, piece, xz_sem.at[src], dev(x, c, y, zt(-1)), group=1)
        send(piece, piece, xx_sem.at[src, 0], dev(xn(1), c, y, z), group=0)
        send(piece, piece, xx_sem.at[src, 1], dev(xn(-1), c, y, z), group=0)

    low, high = pl.ds(0, feats // 2), pl.ds(feats // 2, feats // 2)

    def ev_xx(step):
        src = zt(step)
        left, right = xb.at[src, xn(-1)], xb.at[src, xn(1)]
        arrived(left, xx_sem.at[src, 0])
        send(left.at[low], left.at[low], xx_sem.at[src, 2], dev(xn(1), c, y, z), group=0)
        arrived(right, xx_sem.at[src, 1])
        send(right.at[high], right.at[high], xx_sem.at[src, 3], dev(xn(-1), c, y, z), group=0)

    my_tok = pl.ds(pl.multiple_of(c * half_tok, 16), half_tok)
    its_tok = pl.ds(pl.multiple_of((1 - c) * half_tok, 16), half_tok)

    def ev_yz(step):
        src = zt(step)
        piece = yb.at[src, my_tok]
        arrived(piece, yz_sem.at[src])
        if step in (-1, -2, -3):
            send(piece, piece, yz_sem.at[src], dev(x, c, y, zt(1)), group=3 if step == -3 else 2)
        send(piece, piece, yy_sem.at[src], dev(x, 1 - c, y, z), group=2)

    def ev_mm(step):
        src = zt(step)
        far = xb.at[src, xn(2)]
        arrived(far.at[low], xx_sem.at[src, 2])
        arrived(far.at[high], xx_sem.at[src, 3])
        arrived(yb.at[src, its_tok], yy_sem.at[src])

        def block(i, carry):
            result = jnp.dot(xb[src, i], yb[src], preferred_element_type=jnp.float32)
            grads[src, pl.ds(pl.multiple_of(i * feats, 16), feats), :] = result.astype(jnp.bfloat16)
            return carry

        lax.fori_loop(0, NX, block, 0)
        done.append(src)

        def products(i, sums):
            rows = pl.ds(pl.multiple_of(i * 16, 16), 16)
            new = grads[src, rows, :].astype(jnp.float32)
            return tuple(
                total + lane_sums(new * (new if old is src else grads[old, rows, :].astype(jnp.float32)))
                for old, total in zip(done, sums)
            )

        zero = jnp.zeros((8, 128), jnp.float32)
        sums = lax.fori_loop(0, grads.shape[1] // 16, products, (zero,) * len(done))
        for old, total in zip(done, sums):
            pairs[src, old] = total
            if old is not src:
                pairs[old, src] = total

    done = []
    xz, xx, yz, mm = ev_xz, ev_xx, ev_yz, ev_mm
    sl, yt = ev_sl, ev_ys
    for event, step in [
        (xz, 0), (sl, 0), (xz, -1), (xz, 1), (sl, 1), (xx, 0), (xz, 2), (xz, 3), (yt, 0), (yt, 1),
        (xx, -1), (xx, 1), (xz, -2), (xz, -3), (xx, 2), (xz, 4), (yz, 0), (yz, 1), (yz, -1), (xx, 3), (xx, -2), (xx, -3),
        (mm, 0), (yz, -2), (xx, 4), (mm, 1), (yz, -3), (mm, -1), (yz, 2), (mm, -2), (yz, 3),
        (mm, 2), (mm, -3), (yz, 4), (mm, 3), (mm, 4),
    ]:
        event(step)

    out_lane = lax.broadcasted_iota(jnp.int32, (8, 128), 1)
    a1[tp] = fold(pairs[...])
    for s in range(1, 2 * NX):
        send(a1.at[tp], a1.at[tp], ar_sem.at[0], (dp, (tp + s) % (2 * NX)), group=4)
    arrived(xb.at[pl.ds(0, 7)], group_sem.at[0])
    arrived(xb.at[0, pl.ds(0, 3)], group_sem.at[1])
    arrived(yb.at[pl.ds(0, 7)], group_sem.at[2])
    arrived(yb.at[0, pl.ds(0, half_tok)], group_sem.at[3])
    drain(pending)
    pending.clear()
    sent = pl.ds(0, 2 * NX - 1)
    arrived(a1.at[sent], ar_sem.at[0])
    a2[z] = jnp.sum(a1[...], axis=0)
    for s in range(1, NZ):
        send(a2.at[z], a2.at[z], ar_sem.at[1], dev(x, c, y, zn(s)), group=5)
    arrived(a1.at[sent], group_sem.at[4])
    arrived(a2.at[pl.ds(0, NZ - 1)], ar_sem.at[1])
    weight = tree_weights(jnp.sum(a2[...], axis=0), (4, 2, 1))

    owner = z // 2 % 2
    is_owner = c == owner
    its_rows = pl.ds(pl.multiple_of(c * feats, 16), feats)
    small = 32
    for s in (1, -1, 2, 0):
        part = yn(s)

        def combine_rows(i, carry):
            total = jnp.zeros((small, cols), jnp.float32)
            rows = pl.ds(pl.multiple_of(part * feats + i * small, 32), small)
            for r in range(NZ):
                total += weight[r:r + 1, :] * grads[r, rows, :].astype(jnp.float32)
            vs[part, pl.ds(pl.multiple_of(i * small, small), small), :] = total.astype(jnp.bfloat16)
            return carry

        lax.fori_loop(0, feats // small, combine_rows, 0)
        if s:
            send(vs.at[part], vr.at[y, its_rows], v_sem.at[y, c], dev(x, owner, part, z), group=6)
        else:
            own_v = pltpu.make_async_copy(vs.at[part], vr.at[y, its_rows], v_sem.at[y, c])
            pl.when(is_owner)(own_v.start)
            last_push = counter[0]
            send(vs.at[part], vr.at[y, its_rows], v_sem.at[y, c], dev(x, owner, part, z),
                 jnp.logical_not(is_owner))
            pending.clear()

    def settle():
        arrived(a2.at[pl.ds(0, NZ - 1)], group_sem.at[5])
        arrived(vs.at[pl.ds(0, NY - 1)], group_sem.at[6])

    block = 2 * feats
    cut = block * 2 // 5
    rest = block - cut

    def kind_of(z_):
        return (z_ + 1) // 2 % 2

    def span_of(n):
        return pl.ds(pl.multiple_of(n * cols, 128), cols)

    def part_a(y_, src, start=0, size=cut):
        return out.at[y_, kind_of(src), pl.ds(start, size), span_of(src // 4)]

    def part_b(y_, src):
        return out.at[y_, kind_of(src), pl.ds(cut, rest), span_of(src // 4)]

    class Gather:
        def __init__(self):
            self.waits = []

        def run(self, events):
            for name, *args in events:
                getattr(self, name)(*args)
            drain(self.waits)

        def go(self, ref, sem, device):
            send(ref, ref, sem, device, waits=self.waits)

        def source_z(self):
            for s in (1, -1):
                self.go(part_b(y, z), bz_sem.at[-s % NZ], dev(x, c, y, zt(s)))

        def source_y(self):
            for s in (1, -1):
                self.go(part_a(y, z), ay_sem.at[0 if s > 0 else 1], dev(x, c, yn(s), z))

        def pass_y(self):
            half = cut // 2
            arrived(part_a(yn(-1), z), ay_sem.at[0])
            self.go(part_a(yn(-1), z, 0, half), ay_sem.at[2], dev(x, c, yn(1), z))
            arrived(part_a(yn(1), z), ay_sem.at[1])
            self.go(part_a(yn(1), z, half, half), ay_sem.at[3], dev(x, c, yn(-1), z))

        def last_y(self):
            half = cut // 2
            arrived(part_a(yn(2), z, 0, half), ay_sem.at[2])
            arrived(part_a(yn(2), z, half, half), ay_sem.at[3])

        def first_z(self, offset):
            for s in (1, -1):
                self.go(part_a(yn(offset), z), az_sem.at[-s % NZ, offset % NY], dev(x, c, y, zt(s)))

        def along_z(self, ref, step, sem_at, opposite):
            arrived(ref, sem_at(step % NZ))
            sign = 1 if step > 0 else -1
            if abs(step) < 3 or (abs(step) == 3 and sign == opposite):
                self.go(ref, sem_at(-(step + sign) % NZ), dev(x, c, y, zt(sign)))

        def b_along_z(self, step):
            self.along_z(part_b(y, zt(-step)), step, lambda i: bz_sem.at[i], 1)

        def a_along_z(self, step, offset):
            self.along_z(
                part_a(yn(offset), zt(-step)), step, lambda i: az_sem.at[i, offset % NY],
                -1 if offset in (0, 1) else 1,
            )

        def turn_y(self, step):
            for s in (1, -1):
                ref = part_b(y, zt(-step))
                self.go(ref, by_sem.at[step % NZ, 0 if s > 0 else 1], dev(x, c, yn(s), z))

        def b_along_y(self, step):
            left, right = part_b(yn(-1), zt(-step)), part_b(yn(1), zt(-step))
            arrived(left, by_sem.at[step % NZ, 0])
            arrived(right, by_sem.at[step % NZ, 1])
            sem = by_sem.at[step % NZ, 2]
            if step in (0, 3, 1, -2):
                self.go(left, sem, dev(x, c, yn(1), z))
            else:
                self.go(right, sem, dev(x, c, yn(-1), z))

        def b_end(self, step):
            arrived(part_b(yn(2), zt(-step)), by_sem.at[step % NZ, 2])

    def owner_part():
        for src in range(NY):
            for k in range(2):
                arrived(vr.at[src, pl.ds(k * feats, feats)], v_sem.at[src, k])
        combos = [(a, b) for a in range(NY) for b in range(a, NY)]
        zero = jnp.zeros((8, 128), jnp.float32)

        def products(i, sums):
            rows = pl.ds(pl.multiple_of(i * 16, 16), 16)
            parts = [vr[r, rows, :].astype(jnp.float32) for r in range(NY)]
            return tuple(
                total + lane_sums(parts[a] * parts[b]) for (a, b), total in zip(combos, sums)
            )

        sums = lax.fori_loop(0, block // 16, products, (zero,) * len(combos))
        out_row = lax.broadcasted_iota(jnp.int32, (8, 128), 0) % NY
        out_col = lax.broadcasted_iota(jnp.int32, (8, 128), 1) % NY
        gram = zero
        for (a, b), total in zip(combos, sums):
            value = jnp.sum(total, axis=(0, 1), keepdims=True)
            spot = ((out_row == a) & (out_col == b)) | ((out_row == b) & (out_col == a))
            gram = jnp.where(spot, value, gram)
        me = x * NY + y
        b1[me] = gram
        for s in range(NX):
            for t in range(NY):
                if s or t:
                    send(b1.at[me], b1.at[me], ar_sem.at[2], dev(xn(s), c, yn(t), z), group=7)
        settle()
        arrived(b1.at[pl.ds(0, NX * NY - 1)], ar_sem.at[2])
        b2[z] = jnp.sum(b1[...], axis=0)
        for s in range(1, NZ):
            send(b2.at[z], b2.at[z], ar_sem.at[3], dev(x, zn(s) // 2 % 2, y, zn(s)), group=8)
        arrived(b1.at[pl.ds(0, NX * NY - 1)], group_sem.at[7])
        arrived(b2.at[pl.ds(0, NZ - 1)], ar_sem.at[3])
        last = tree_weights(jnp.sum(b2[...], axis=0), (2, 1))
        side, n = kind_of(z), z // 4
        span = span_of(n)

        def final_rows(i, carry):
            total = jnp.zeros((small, cols), jnp.float32)
            rows = pl.ds(pl.multiple_of(i * small, small), small)
            for r in range(NY):
                total += last[r:r + 1, :] * vr[r, rows, :].astype(jnp.float32)
            out[y, side, rows, span] = total.astype(jnp.bfloat16)
            return carry

        lax.fori_loop(0, block // small, final_rows, 0)
        arrived(b2.at[pl.ds(0, NZ - 1)], group_sem.at[8])
        Gather().run(OWNER_EVENTS)

    def other_part():
        settle()
        arrived(vs.at[0], send_sem.at[last_push])
        Gather().run(OTHER_EVENTS)

    pl.when(is_owner)(owner_part)
    pl.when(jnp.logical_not(is_owner))(other_part)


def on_device(tokens, pre_act, act_grad):
    tok, feat = tokens.shape
    width = pre_act.shape[1]
    feats, cols = feat // 2, width // 2
    rows = feats * NX
    bf16, f32 = jnp.bfloat16, jnp.float32
    dma = pltpu.SemaphoreType.DMA
    combined = pl.pallas_call(
        kernel,
        out_shape=pltpu.VMEM((NX, 2, feat, width), bf16),
        in_specs=[
            pl.BlockSpec(memory_space=pl.ANY),
            pl.BlockSpec(memory_space=pl.ANY),
            pl.BlockSpec(memory_space=pl.ANY),
        ],
        out_specs=pl.BlockSpec(memory_space=pltpu.VMEM),
        scratch_shapes=[
            pltpu.VMEM((NZ, NX, feats, tok), bf16),
            pltpu.VMEM((NZ, tok, cols), bf16),
            pltpu.VMEM((2, tok, cols), bf16),
            pltpu.VMEM((tok, width), bf16),
            pltpu.VMEM((tok, width), bf16),
            pltpu.VMEM((NZ, rows, cols), bf16),
            pltpu.VMEM((NZ, NZ, 8, 128), f32),
            pltpu.VMEM((NY, feats, cols), bf16),
            pltpu.VMEM((NY, 2 * feats, cols), bf16),
            pltpu.VMEM((2 * NX, 8, 128), f32),
            pltpu.VMEM((NZ, 8, 128), f32),
            pltpu.VMEM((NX * NY, 8, 128), f32),
            pltpu.VMEM((NZ, 8, 128), f32),
            dma((2,)),
            dma((SEND_SEMS,)),
            dma((9,)),
            dma((NZ,)),
            dma((NZ, 4)),
            dma((NZ,)),
            dma((NZ,)),
            dma((NY, 2)),
            dma((4,)),
            dma((NZ,)),
            dma((NZ, 3)),
            dma((NZ, NY)),
            dma((4,)),
        ],
        compiler_params=pltpu.CompilerParams(
            collective_id=0, has_side_effects=True, vmem_limit_bytes=52 * 1024 * 1024
        ),
    )(tokens.T, pre_act, act_grad)
    return combined.reshape(feat * 2 * NX, width)


def solution(mesh):
    return jax.shard_map(
        on_device,
        mesh=mesh,
        in_specs=(P("dp", "tp"), P("dp", "tp"), P("dp", "tp")),
        out_specs=P(None, "tp"),
        check_vma=False,
    )
```

time: 174 us -> 165 us (0.948)
  the two profiles are of different devices: /device:TPU:32 before, /device:TPU:1 now
where the time goes in v3:
time: 165 us; the launch traced here: 161 us
  Pallas kernels  158 us (96%)
  local copies, waits for them, and re-layouts  2.79 us (2%)
    pallas_call x1, Pallas kernels, on_device(): pl.pallas_call(kernel, out_shape=pltpu.VMEM((NX, 2, feat, width), bf16),...  158 us

profile of v3, /device:TPU:1, one launch (start us, length us, event | category | flops | bytes accessed | tf_op | source)
XLA Modules:
  0.0 161.3 jit_solution(3945856466277882527)
XLA Ops:
  0.0 158.5 %shard_map.37 = bf16[4,2,320,1280]{3,2,1,0:T(8,128)(2,1)S(1)} custom-call(bf16[320,512]{1,0:T(8,128)(2,1)} %bitcast.3, bf16[512,1280]{1,0:T(8,128)(2,1)} %pre.1, bf16[512,1280]{1,0:T(8,128)(2,1)} %act.1), custom_call_target="tpu_custom_call" | custom-call | tf_op jit(solution)/shard_map/pallas_call | solution.py:487
  158.5 2.8 %copy.5 = bf16[2560,1280]{1,0:T(8,128)(2,1)} copy(bf16[2560,1280]{1,0:T(8,128)(2,1)S(1)} %bitcast.2) | data formatting | bytes 13107200

commit v4 on v3

--- a/solution.py
+++ b/solution.py
@@ -70,24 +70,9 @@
     return total[:8] + total[8:]
 
 
-def exact_dot(left, right):
-    return jnp.dot(
-        left, right, preferred_element_type=jnp.float32, precision=lax.Precision.HIGHEST
-    )
-
-
-def fold(sums):
-    size = sums.shape[0] * sums.shape[1] * sums.shape[2]
-    across = exact_dot(sums.reshape(size, 128), jnp.ones((128, 128), jnp.float32))
-    row = lax.broadcasted_iota(jnp.int32, (size, 128), 0)
-    lane = lax.broadcasted_iota(jnp.int32, (size, 128), 1)
-    kept = jnp.where(row // 8 % 8 == lane % 8, across, 0.0)
-    return jnp.sum(kept.reshape(8, size // 8, 128), axis=1)
-
-
 def kernel(
     xt, pre, act, out,
-    xb, yb, ys, pre_v, act_v, grads, pairs, vs, vr,
+    xb, yb, ys, pre_v, act_v, grads, vs, vr,
     a1, a2, b1, b2,
     load_sem, send_sem, group_sem, xz_sem, xx_sem, yz_sem, yy_sem, v_sem, ar_sem,
     bz_sem, by_sem, az_sem, ay_sem,
@@ -251,7 +236,9 @@
 
         def block(i, carry):
             result = jnp.dot(xb[src, i], yb[src], preferred_element_type=jnp.float32)
-            grads[src, pl.ds(pl.multiple_of(i * feats, 16), feats), :] = result.astype(jnp.bfloat16)
+            grads[src, pl.ds(pl.multiple_of(i * feats, 16), feats), :] = result.astype(
+                jnp.bfloat16
+            ).astype(jnp.float32)
             return carry
 
         lax.fori_loop(0, NX, block, 0)
@@ -259,20 +246,23 @@
 
         def products(i, sums):
             rows = pl.ds(pl.multiple_of(i * 16, 16), 16)
-            new = grads[src, rows, :].astype(jnp.float32)
+            new = grads[src, rows, :]
             return tuple(
-                total + lane_sums(new * (new if old is src else grads[old, rows, :].astype(jnp.float32)))
+                total + lane_sums(new * (new if old is src else grads[old, rows, :]))
                 for old, total in zip(done, sums)
             )
 
         zero = jnp.zeros((8, 128), jnp.float32)
         sums = lax.fori_loop(0, grads.shape[1] // 16, products, (zero,) * len(done))
         for old, total in zip(done, sums):
-            pairs[src, old] = total
-            if old is not src:
-                pairs[old, src] = total
+            value = jnp.sum(total, axis=(0, 1), keepdims=True)
+            spot = ((lead == src) & (tail == old)) | ((lead == old) & (tail == src))
+            gram[0] = jnp.where(spot, value, gram[0])
 
     done = []
+    gram = [jnp.zeros((8, 128), jnp.float32)]
+    lead = lax.broadcasted_iota(jnp.int32, (8, 128), 0)
+    tail = lax.broadcasted_iota(jnp.int32, (8, 128), 1) % NZ
     xz, xx, yz, mm = ev_xz, ev_xx, ev_yz, ev_mm
     sl, yt = ev_sl, ev_ys
     for event, step in [
@@ -283,8 +273,7 @@
     ]:
         event(step)
 
-    out_lane = lax.broadcasted_iota(jnp.int32, (8, 128), 1)
-    a1[tp] = fold(pairs[...])
+    a1[tp] = gram[0]
     for s in range(1, 2 * NX):
         send(a1.at[tp], a1.at[tp], ar_sem.at[0], (dp, (tp + s) % (2 * NX)), group=4)
     arrived(xb.at[pl.ds(0, 7)], group_sem.at[0])
@@ -313,7 +302,7 @@
             total = jnp.zeros((small, cols), jnp.float32)
             rows = pl.ds(pl.multiple_of(part * feats + i * small, 32), small)
             for r in range(NZ):
-                total += weight[r:r + 1, :] * grads[r, rows, :].astype(jnp.float32)
+                total += weight[r:r + 1, :] * grads[r, rows, :]
             vs[part, pl.ds(pl.multiple_of(i * small, small), small), :] = total.astype(jnp.bfloat16)
             return carry
 
@@ -499,8 +488,7 @@
             pltpu.VMEM((2, tok, cols), bf16),
             pltpu.VMEM((tok, width), bf16),
             pltpu.VMEM((tok, width), bf16),
-            pltpu.VMEM((NZ, rows, cols), bf16),
-            pltpu.VMEM((NZ, NZ, 8, 128), f32),
+            pltpu.VMEM((NZ, rows, cols), f32),
             pltpu.VMEM((NY, feats, cols), bf16),
             pltpu.VMEM((NY, 2 * feats, cols), bf16),
             pltpu.VMEM((2 * NX, 8, 128), f32),

time: 165 us -> 163 us (0.988)
  no operation moved by 1% of the time
where the time goes in v4:
time: 163 us; the launch traced here: 160 us
  Pallas kernels  157 us (96%)
  local copies, waits for them, and re-layouts  2.79 us (2%)
    pallas_call x1, Pallas kernels, on_device(): pl.pallas_call(kernel, out_shape=pltpu.VMEM((NX, 2, feat, width), bf16),...  157 us

profile of v4, /device:TPU:1, one launch (start us, length us, event | category | flops | bytes accessed | tf_op | source)
XLA Modules:
  0.0 159.9 jit_solution(3972705197434076880)
XLA Ops:
  0.0 157.1 %shard_map.37 = bf16[4,2,320,1280]{3,2,1,0:T(8,128)(2,1)S(1)} custom-call(bf16[320,512]{1,0:T(8,128)(2,1)} %bitcast.3, bf16[512,1280]{1,0:T(8,128)(2,1)} %pre.1, bf16[512,1280]{1,0:T(8,128)(2,1)} %act.1), custom_call_target="tpu_custom_call" | custom-call | tf_op jit(solution)/shard_map/pallas_call | solution.py:476
  157.1 2.8 %copy.5 = bf16[2560,1280]{1,0:T(8,128)(2,1)} copy(bf16[2560,1280]{1,0:T(8,128)(2,1)S(1)} %bitcast.2) | data formatting | bytes 13107200

commit v5 on v4

--- a/solution.py
+++ b/solution.py
@@ -295,7 +295,7 @@
     is_owner = c == owner
     its_rows = pl.ds(pl.multiple_of(c * feats, 16), feats)
     small = 32
-    for s in (1, -1, 2, 0):
+    for s in (2, 1, -1, 0):
         part = yn(s)
 
         def combine_rows(i, carry):

time: 163 us -> 163 us (level)
  no operation moved by 1% of the time
where the time goes in v5:
time: 163 us; the launch traced here: 160 us
  Pallas kernels  157 us (96%)
  local copies, waits for them, and re-layouts  2.79 us (2%)
    pallas_call x1, Pallas kernels, on_device(): pl.pallas_call(kernel, out_shape=pltpu.VMEM((NX, 2, feat, width), bf16),...  157 us

profile of v5, /device:TPU:1, one launch (start us, length us, event | category | flops | bytes accessed | tf_op | source)
XLA Modules:
  0.0 160.2 jit_solution(897684466940515448)
XLA Ops:
  0.0 157.4 %shard_map.37 = bf16[4,2,320,1280]{3,2,1,0:T(8,128)(2,1)S(1)} custom-call(bf16[320,512]{1,0:T(8,128)(2,1)} %bitcast.3, bf16[512,1280]{1,0:T(8,128)(2,1)} %pre.1, bf16[512,1280]{1,0:T(8,128)(2,1)} %act.1), custom_call_target="tpu_custom_call" | custom-call | tf_op jit(solution)/shard_map/pallas_call | solution.py:476
  157.4 2.8 %copy.5 = bf16[2560,1280]{1,0:T(8,128)(2,1)} copy(bf16[2560,1280]{1,0:T(8,128)(2,1)S(1)} %bitcast.2) | data formatting | bytes 13107200
